TPU v7x, 128 devices: a whole 4x4x4 slice. The times are simulated.
128 devices in a mesh: tm: 16 (over z_hi, x, core), height: 8 (over z_lo, y).
Axes of the slice: x: 4, y: 4, z: 4 (z_hi: 2, z_lo: 2; z = z_hi * 2 + z_lo), core: 2. Of those that a mesh axis runs over, the one named last changes fastest.
Arguments:
- coarse: bfloat16 [8, 32, 128, 256], P('height', 'tm'), may hold values from -360 to 360
- gain: float32 [256], replicated, may hold values from 0.1 to 1.9
- bias: float32 [256], replicated, may hold values from -3 to 3
- weight: bfloat16 [256, 3, 3, 3, 128], replicated, may hold values from -0.078125 to 0.078125
- cotangent: bfloat16 [8, 64, 256, 128], P(None, 'tm', 'height'), may hold values from -0.0390625 to 0.0390625
Outputs:
- decoded: bfloat16 [8, 64, 256, 128], P(None, 'tm', 'height')
- grad_weight: float32 [256, 3, 3, 3, 128], P('tm')
- grad_affine: float32 [2, 256], replicated
All inputs are finite; a program needn't handle non-finite values.
Results may differ from a plain program's by a relative error of at most 0.0051.
Values may be sent and summed in bfloat16 or wider, within the bound.
A program may use at most 64 MiB of HBM per device.

v0:
```python
import jax
import jax.numpy as jnp
from jax import lax
from jax.sharding import PartitionSpec as P

GROUPS = 32


EPSILON = 1e-06


def extended_2(block, sides, width):
    for axis, dim in sides:
        count = lax.axis_size(axis)
        forward = [(i, i + 1) for i in range(count - 1)]
        backward = [(target, source) for source, target in forward]
        low = lax.ppermute(
            lax.slice_in_dim(block, block.shape[dim] - width, None, axis=dim), axis, forward
        )
        high = lax.ppermute(lax.slice_in_dim(block, 0, width, axis=dim), axis, backward)
        block = jnp.concatenate([low, block, high], axis=dim)
    return block


def per_device(coarse, gain, bias, weight, cotangent):
    channels_in = coarse.shape[3]
    grouped = coarse.astype(jnp.float32).reshape(coarse.shape[:3] + (GROUPS, channels_in // GROUPS))
    partial_sums = (
        jnp.sum(grouped, axis=(0, 1, 2, 4)),
        jnp.sum(grouped * grouped, axis=(0, 1, 2, 4)),
    )
    totals, squares = lax.psum((partial_sums[0], partial_sums[1]), ("tm", "height"))
    numbers = (
        grouped.shape[0]
        * grouped.shape[1]
        * grouped.shape[2]
        * grouped.shape[4]
        * lax.axis_size("tm")
        * lax.axis_size("height")
    )
    average = totals / numbers
    variance = squares / numbers - average * average
    inverse = lax.rsqrt(variance + EPSILON)
    spread = coarse.astype(jnp.float32).reshape(coarse.shape[:3] + (GROUPS, channels_in // GROUPS))
    normed = ((spread - average[:, None]) * inverse[:, None]).reshape(coarse.shape)
    normed, shifted = (normed, normed * gain + bias)
    activation = lax.all_to_all(
        jax.nn.silu(shifted).astype(jnp.bfloat16), "height", split_axis=2, concat_axis=0, tiled=True
    )
    extended = extended_2(activation, (("tm", 1), ("height", 2)), 1)
    upsampled = jnp.repeat(jnp.repeat(extended, 2, axis=1), 2, axis=2)[:, 1:-1, 1:-1]
    upsampled = jnp.pad(upsampled, ((2, 0), (0, 0), (0, 0), (0, 0)))
    frames_here, rows_here, cols_here, channels_out = cotangent.shape
    flat_cot = cotangent.reshape(-1, channels_out)
    cot_ext = extended_2(cotangent, (("tm", 1), ("height", 2)), 1)
    cot_ext = jnp.pad(cot_ext, ((0, 2), (0, 0), (0, 0), (0, 0)))
    product = jnp.zeros((frames_here * rows_here * cols_here, channels_out), jnp.float32)
    grad_up = jnp.zeros((frames_here * rows_here * cols_here, channels_in), jnp.float32)
    for tap_t in range(3):
        for tap_r in range(3):
            for tap_c in range(3):
                window = upsampled[
                    tap_t : tap_t + frames_here,
                    tap_r : tap_r + rows_here,
                    tap_c : tap_c + cols_here,
                ].reshape(-1, channels_in)
                kernel = weight[:, tap_t, tap_r, tap_c, :]
                product = product + jnp.dot(window, kernel, preferred_element_type=jnp.float32)
                cot_window = cot_ext[
                    2 - tap_t : 2 - tap_t + frames_here,
                    2 - tap_r : 2 - tap_r + rows_here,
                    2 - tap_c : 2 - tap_c + cols_here,
                ].reshape(-1, channels_out)
                grad_up = grad_up + lax.dot_general(
                    cot_window, kernel, (((1,), (1,)), ((), ())), preferred_element_type=jnp.float32
                )
    decoded = product.reshape(cotangent.shape).astype(jnp.bfloat16)
    pieces = []
    for tap_t in range(3):
        for tap_r in range(3):
            for tap_c in range(3):
                window = upsampled[
                    tap_t : tap_t + frames_here,
                    tap_r : tap_r + rows_here,
                    tap_c : tap_c + cols_here,
                ]
                window = window.reshape(-1, channels_in)
                pieces.append(
                    lax.dot_general(
                        window,
                        flat_cot,
                        (((0,), (0,)), ((), ())),
                        preferred_element_type=jnp.float32,
                    )
                )
    full_term = lax.psum(
        jnp.stack(pieces, axis=1).reshape(channels_in, 3, 3, 3, channels_out), "height"
    )
    grad_weight = lax.psum_scatter(full_term, "tm", scatter_dimension=0, tiled=True)
    grad_act = grad_up.reshape(frames_here, rows_here // 2, 2, cols_here // 2, 2, channels_in).sum(
        axis=(2, 4)
    )
    grad_act = lax.all_to_all(grad_act, "height", split_axis=0, concat_axis=2, tiled=True)
    sigmoid_z = jax.nn.sigmoid(shifted)
    grad_shifted = grad_act * sigmoid_z * (1.0 + shifted * (1.0 - sigmoid_z))
    gain_part, bias_part = lax.psum(
        (jnp.sum(grad_shifted * normed, axis=(0, 1, 2)), jnp.sum(grad_shifted, axis=(0, 1, 2))),
        ("tm", "height"),
    )
    grad_affine = jnp.stack([gain_part, bias_part])
    return (decoded, grad_weight, grad_affine)


def solution(mesh):
    return jax.shard_map(
        per_device,
        mesh=mesh,
        in_specs=(P("height", "tm", None, None), P(), P(), P(), P(None, "tm", "height", None)),
        out_specs=(P(None, "tm", "height", None), P("tm", None, None, None, None), P()),
        check_vma=False,
    )
```

profile of v0, /device:TPU:0, one launch (start us, length us, event | category | flops | bytes accessed | tf_op | source)
XLA Modules:
  0.0 411.1 jit_solution(17213361920708432055)
XLA Ops:
  7.2 1.0 fusion.180
  8.2 1.3 collective-permute-start.4
  9.5 1.3 collective-permute-start.5
  10.8 3.6 collective-permute-done.5
  14.4 1.2 pad_maximum_fusion.4
  15.8 1.3 collective-permute-start.7
  17.1 4.5 %collective-permute-start.6 = (bf16[8,6,1,128]{3,2,1,0:T(2,128)(2,1)S(1)}, bf16[8,6,1,128]{3,2,1,0:T(2,128)(2,1)S(1)}, u32[]{:S(2)}, u32[]{:S(2)}) collective-permute-start(bf16[8,6,1,128]{3,2,1,0:T(2,128)(2,1)S(1)} %get-tuple-element.66), channel_id=1, source_target_pairs={{0,1},{1,2},{2,3},{3,4},{4,5},{5,6},{6,7},{8,9},{9,10},{10,11},{11... | collective-permute-start | bytes 36872 | tf_op jit(solution)/shard_map/ppermute | solution.py:17
  21.9 1.2 collective-permute-done.6
  24.6 1.1 fusion.178
  33.7 1.6 reshape.317
  35.3 2.7 reduce_sum.65
  38.1 8.1 %all-to-all-start.1 = ((f32[8,2,16,256]{3,2,1,0:T(8,128)}), f32[8,2,16,256]{3,2,1,0:T(8,128)S(1)}, u32[]{:S(2)}, u32[]{:S(2)}) async-start(f32[8,2,16,256]{3,2,1,0:T(8,128)} %reduce_sum.65), calls=%async_computation.1 | async-start | bytes 524288 | tf_op jit(solution)/shard_map/all_to_all | solution.py:103
  46.7 72.6 %all-reduce.3 = (f32[32]{0:T(128)S(1)}, f32[32]{0:T(128)S(1)}) all-reduce(f32[32]{0:T(128)S(1)} %reduce_sum.64, f32[32]{0:T(128)S(1)} %reduce_sum.61), channel_id=1, replica_groups=mesh['tm'=16,'height'=8] {'tm','height'}, use_global_device_ids=true, to_apply=%region_5.6 | all-reduce | flops 64 | bytes 512 | tf_op jit(solution)/shard_map/psum | solution.py:32
  120.0 10.0 %all_to_all.36 = bf16[1,2,128,256]{3,1,0,2:T(2,128)(2,1)S(1)} all-to-all(bf16[1,2,128,256]{3,1,0,2:T(2,128)(2,1)S(1)} %copy.32), channel_id=1, replica_groups=mesh['tm'=16,'height'=8] {'height'}, dimensions={2} | all-to-all | bytes 262144 | tf_op jit(solution)/shard_map/all_to_all | solution.py:47
  130.3 1.3 collective-permute-start.1
  131.6 3.0 collective-permute-start
  134.7 65.8 %all-reduce.2 = (f32[1,256]{1,0:T(1,128)S(1)}, f32[1,256]{1,0:T(1,128)S(1)}) all-reduce(f32[1,256]{1,0:T(1,128)S(1)} %bitcast.567, f32[1,256]{1,0:T(1,128)S(1)} %bitcast.566), channel_id=1, replica_groups=mesh['tm'=16,'height'=8] {'tm','height'}, use_global_device_ids=true, to_apply=%region_12.13 | all-reduce | flops 512 | bytes 4096 | tf_op jit(solution)/shard_map/psum | solution.py:106
  200.6 1.3 collective-permute-start.3
  201.9 4.5 %collective-permute-start.2 = (bf16[8,4,1,256]{3,1,2,0:T(4,128)(2,1)S(1)}, bf16[8,4,1,256]{3,1,2,0:T(4,128)(2,1)S(1)}, u32[]{:S(2)}, u32[]{:S(2)}) collective-permute-start(bf16[8,4,1,256]{3,1,2,0:T(4,128)(2,1)S(1)} %get-tuple-element.67), channel_id=1, source_target_pairs={{0,1},{1,2},{2,3},{3,4},{4,5},{5,6},{6,7},{8,9},{9,10},{10,11},{11... | collective-permute-start | bytes 49160 | tf_op jit(solution)/shard_map/ppermute | solution.py:17
  209.3 2.9 fusion.177
  212.4 4.1 %pad_slice_fusion = (bf16[8,4,32,256]{3,2,1,0:T(8,128)(2,1)S(1)}, bf16[8,4,32,256]{3,2,1,0:T(8,128)(2,1)}, bf16[8,4,32,256]{3,2,1,0:T(8,128)(2,1)}, bf16[8,4,32,...) fusion(bf16[8,6,34,256]{3,2,1,0:T(8,128)(2,1)S(1)} %copy.71), kind=kLoop, calls=%fused_computation.111 | loop fusion | bytes 10272768 | tf_op jit(solution)/shard_map/slice | solution.py:62
  217.5 1.1 fusion.112
  229.8 1.0 fusion.29
  231.7 1.0 fusion.27
  232.7 1.0 fusion.26
  234.6 1.0 fusion.24
  235.6 1.0 fusion.23
  236.6 1.0 fusion.22
  237.6 1.0 fusion.21
  238.6 1.0 fusion.20
  239.6 1.0 fusion.19
  240.6 1.0 fusion.18
  241.6 1.0 fusion.17
  242.6 1.0 fusion.16
  243.6 1.0 fusion.15
  244.6 1.0 fusion.14
  245.6 1.0 fusion.13
  246.6 1.0 fusion.12
  247.6 1.0 fusion.11
  248.6 1.0 fusion.10
  249.6 1.0 fusion.9
  250.6 1.0 fusion.8
  251.6 1.0 fusion.7
  252.9 1.6 convolution_add_fusion.48
  265.2 64.3 %reduce-scatter.2.cloned.1.call-done = f32[16,3,3,3,128]{4,0,3,2,1:T(8,128)} async-done(((f32[256,3,3,3,128]{4,0,3,2,1:T(8,128)}), f32[16,3,3,3,128]{4,0,3,2,1:T(8,128)}) %reduce-scatter.2.cloned.1.call-update) | async-done | bytes 221200 | tf_op jit(solution)/shard_map/reduce_scatter | solution.py:99
  329.5 1.0 fusion.6
  330.5 72.0 %all-reduce.6.cloned.1.call-done = f32[16,3,3,3,128]{4,0,3,2,1:T(8,128)} async-done(((f32[16,3,3,3,128]{4,0,3,2,1:T(8,128)}), f32[16,3,3,3,128]{4,0,3,2,1:T(8,128)}) %all-reduce.6.cloned.1.call-update) | async-done | bytes 221200 | tf_op jit(solution)/shard_map/psum | solution.py:96
  402.6 1.6 copy.128
  (161 shorter events, 38.9 us)
Async XLA Ops:
  7.2 14.4 %copy-start = (bf16[256,3,3,3,128]{4,0,3,2,1:T(8,128)(2,1)S(1)}, bf16[256,3,3,3,128]{4,0,3,2,1:T(8,128)(2,1)}, u32[]{:S(2)}) copy-start(bf16[256,3,3,3,128]{4,0,3,2,1:T(8,128)(2,1)} %param.8) | copy-start | bytes 5308420
  8.2 2.6 collective-permute-start.4
  9.5 5.0 %collective-permute-start.5 = (bf16[8,1,32,128]{3,2,1,0:T(8,128)(2,1)S(1)}, bf16[8,1,32,128]{3,2,1,0:T(8,128)(2,1)S(1)}, u32[]{:S(2)}, u32[]{:S(2)}) collective-permute-start(bf16[8,1,32,128]{3,2,1,0:T(8,128)(2,1)S(1)} %get-tuple-element.72), channel_id=1, source_target_pairs={{8,0},{16,8},{24,16},{32,24},{40,32},{48,40},{56,48},{64,56},{72,6... | collective-permute-start | bytes 196616 | tf_op jit(solution)/shard_map/ppermute | solution.py:20
  15.8 6.2 %collective-permute-start.7 = (bf16[8,6,1,128]{3,2,1,0:T(2,128)(2,1)S(1)}, bf16[8,6,1,128]{3,2,1,0:T(2,128)(2,1)S(1)}, u32[]{:S(2)}, u32[]{:S(2)}) collective-permute-start(bf16[8,6,1,128]{3,2,1,0:T(2,128)(2,1)S(1)} %get-tuple-element.65), channel_id=1, source_target_pairs={{1,0},{2,1},{3,2},{4,3},{5,4},{6,5},{7,6},{9,8},{10,9},{11,10},{12... | collective-permute-start | bytes 36872 | tf_op jit(solution)/shard_map/ppermute | solution.py:20
  17.1 6.1 %collective-permute-start.6 = (bf16[8,6,1,128]{3,2,1,0:T(2,128)(2,1)S(1)}, bf16[8,6,1,128]{3,2,1,0:T(2,128)(2,1)S(1)}, u32[]{:S(2)}, u32[]{:S(2)}) collective-permute-start(bf16[8,6,1,128]{3,2,1,0:T(2,128)(2,1)S(1)} %get-tuple-element.66), channel_id=1, source_target_pairs={{0,1},{1,2},{2,3},{3,4},{4,5},{5,6},{6,7},{8,9},{9,10},{10,11},{11... | collective-permute-start | bytes 36872 | tf_op jit(solution)/shard_map/ppermute | solution.py:17
  31.8 1.0 copy-start.23
  33.7 12.6 %copy-start.25 = (bf16[1,2,128,256]{3,2,1,0:T(8,128)(2,1)S(1)}, bf16[1,2,128,256]{3,2,1,0:T(8,128)(2,1)}, u32[]{:S(2)}) copy-start(bf16[1,2,128,256]{3,2,1,0:T(8,128)(2,1)} %param.5) | copy-start | bytes 393220
  35.3 84.4 %copy-start.26 = (f32[256]{0:T(256)S(1)}, f32[256]{0:T(256)}, u32[]{:S(2)}) copy-start(f32[256]{0:T(256)} %param.7) | copy-start | bytes 3076
  35.3 84.4 %copy-start.27 = (f32[256]{0:T(256)S(1)}, f32[256]{0:T(256)}, u32[]{:S(2)}) copy-start(f32[256]{0:T(256)} %param.6) | copy-start | bytes 3076
  38.1 81.6 %all-to-all-start.1 = ((f32[8,2,16,256]{3,2,1,0:T(8,128)}), f32[8,2,16,256]{3,2,1,0:T(8,128)S(1)}, u32[]{:S(2)}, u32[]{:S(2)}) async-start(f32[8,2,16,256]{3,2,1,0:T(8,128)} %reduce_sum.65), calls=%async_computation.1 | async-start | bytes 524288 | tf_op jit(solution)/shard_map/all_to_all | solution.py:103
  46.2 283.3 %reduce-scatter.2.cloned.1.call-start = ((), (), s32[]{:S(2)}) async-start(), calls=%async_computation.3 | async-start | bytes 3760128 | tf_op jit(solution)/shard_map/reduce_scatter | solution.py:99
  130.3 70.2 %collective-permute-start.1 = (bf16[8,1,16,256]{3,1,2,0:T(2,128)(2,1)S(1)}, bf16[8,1,16,256]{3,1,2,0:T(2,128)(2,1)S(1)}, u32[]{:S(2)}, u32[]{:S(2)}) collective-permute-start(bf16[8,1,16,256]{3,1,2,0:T(2,128)(2,1)S(1)} %get-tuple-element.77), channel_id=1, source_target_pairs={{8,0},{16,8},{24,16},{32,24},{40,32},{48,40},{56,48},{64,56},{72,6... | collective-permute-start | bytes 196616 | tf_op jit(solution)/shard_map/ppermute | solution.py:20
  131.6 69.0 %collective-permute-start = (bf16[8,1,16,256]{3,1,2,0:T(2,128)(2,1)S(1)}, bf16[8,1,16,256]{3,1,2,0:T(2,128)(2,1)S(1)}, u32[]{:S(2)}, u32[]{:S(2)}) collective-permute-start(bf16[8,1,16,256]{3,1,2,0:T(2,128)(2,1)S(1)} %get-tuple-element.76), channel_id=1, source_target_pairs={{0,8},{8,16},{16,24},{24,32},{32,40},{40,48},{48,56},{56,64},{64,7... | collective-permute-start | bytes 196616 | tf_op jit(solution)/shard_map/ppermute | solution.py:17
  200.6 6.4 %collective-permute-start.3 = (bf16[8,4,1,256]{3,1,2,0:T(4,128)(2,1)S(1)}, bf16[8,4,1,256]{3,1,2,0:T(4,128)(2,1)S(1)}, u32[]{:S(2)}, u32[]{:S(2)}) collective-permute-start(bf16[8,4,1,256]{3,1,2,0:T(4,128)(2,1)S(1)} %get-tuple-element.68), channel_id=1, source_target_pairs={{1,0},{2,1},{3,2},{4,3},{5,4},{6,5},{7,6},{9,8},{10,9},{11,10},{12... | collective-permute-start | bytes 49160 | tf_op jit(solution)/shard_map/ppermute | solution.py:20
  201.9 6.0 %collective-permute-start.2 = (bf16[8,4,1,256]{3,1,2,0:T(4,128)(2,1)S(1)}, bf16[8,4,1,256]{3,1,2,0:T(4,128)(2,1)S(1)}, u32[]{:S(2)}, u32[]{:S(2)}) collective-permute-start(bf16[8,4,1,256]{3,1,2,0:T(4,128)(2,1)S(1)} %get-tuple-element.67), channel_id=1, source_target_pairs={{0,1},{1,2},{2,3},{3,4},{4,5},{5,6},{6,7},{8,9},{9,10},{10,11},{11... | collective-permute-start | bytes 49160 | tf_op jit(solution)/shard_map/ppermute | solution.py:17
  212.4 4.1 %copy-start.24 = (bf16[8,4,32,128]{3,2,1,0:T(8,128)(2,1)S(1)}, bf16[8,4,32,128]{3,2,1,0:T(8,128)(2,1)}, u32[]{:S(2)}) copy-start(bf16[8,4,32,128]{3,2,1,0:T(8,128)(2,1)} %param.9) | copy-start | bytes 786436
  252.6 149.9 %all-reduce.6.cloned.1.call-start = ((), (), s32[]{:S(2)}) async-start(), calls=%async_computation.4 | async-start | bytes 442368 | tf_op jit(solution)/shard_map/psum | solution.py:96
  252.9 1.6 copy-start.13
  252.9 1.9 copy-start.12
  254.5 1.0 copy-start.11
  254.8 1.1 copy-start.10
  255.1 1.1 copy-start.9
  255.8 1.1 copy-start.8
  256.2 1.1 copy-start.7
  256.6 1.1 copy-start.6
  257.2 1.1 copy-start.5
  257.6 1.1 copy-start.4
  258.0 1.1 copy-start.3
  258.6 1.1 copy-start.2
  259.0 1.1 copy-start.1
  260.7 1.1 copy-start.21
  261.0 1.1 copy-start.20
  261.3 1.1 copy-start.19
  262.1 1.1 copy-start.18
  262.4 1.1 copy-start.17
  262.8 1.1 copy-start.16
  263.5 1.1 copy-start.15
  263.8 1.1 copy-start.14
  264.2 65.3 %copy-start.22 = (bf16[8,4,32,256]{3,2,1,0:T(8,128)(2,1)S(1)}, bf16[8,4,32,256]{3,2,1,0:T(8,128)(2,1)}, u32[]{:S(2)}) copy-start(bf16[8,4,32,256]{3,2,1,0:T(8,128)(2,1)} %copy.80) | copy-start | bytes 1572868
Sparse Core Ops, SparseCore 0:
  252.8 76.6 reduce-scatter.1
  332.0 70.5 all-reduce.5
where the time goes:
time: 412 us; the launch traced here: 411 us
  blocking collectives  148 us (36%)
  waiting for transfers between devices  142 us (34%)
  matrix products  45.5 us (11%)
  starting transfers between devices  27 us (7%)
  local copies, waits for them, and re-layouts  26.8 us (7%)
  between operations  14.8 us (4%)
  other arithmetic  6.43 us (2%)
    psum x1, blocking collectives, per_device(): lax.psum((partial_sums[0], partial_sums[1]), ('tm', 'height'))  72.6 us
    psum x1, waiting for transfers between devices, per_device(): lax.psum(jnp.stack(pieces, axis=1).reshape(channels_in, 3, 3, 3, channels...  72 us
    psum x1, blocking collectives, per_device(): lax.psum((jnp.sum(grad_shifted * normed, axis=(0, 1, 2)), jnp.sum(grad_sh...  65.8 us
    reduce_scatter x1, waiting for transfers between devices, per_device(): lax.psum_scatter(full_term, 'tm', scatter_dimension=0, tiled=True)  64.3 us
    dot_general x27, matrix products, per_device(): lax.dot_general(window, flat_cot, (((0,), (0,)), ((), ())), preferred_ele...  26.7 us
    unnamed x68, local copies, waits for them, and re-layouts  14.1 us
    ppermute x4, starting transfers between devices, extended_2(): lax.ppermute(lax.slice_in_dim(block, block.shape[dim] - width, None, axis...  13.4 us
    dot_general x27, matrix products, per_device(): jnp.dot(window, kernel, preferred_element_type=jnp.float32)  10.8 us
  transfers between devices with their start and end apart: 11, of which 5 were waited for; matrix products, arithmetic and copies ran while one was open for 3% of the time, Pallas kernels for 0%

commit v1 on v0

v1 whole, which is shorter than its diff:
```python
import functools

import jax
import jax.numpy as jnp
from jax import lax
from jax.experimental import pallas as pl
from jax.experimental.pallas import tpu as pltpu
from jax.sharding import PartitionSpec as P

MESH = pl.DeviceIdType.MESH
F32, BF16 = jnp.float32, jnp.bfloat16
EPSILON = 1e-06
NUMBERS = 8 * 32 * 128 * 8
CHIPS, HEIGHT = 8, 8

(STATS1, STATS2, BLOCKS, COT_PAIR, COT_ROWS, COT_COLS, X_PAIR, X_ROWS, X_COLS, REDUCE, GATHER, AFF1, AFF2) = range(13)


def group_totals(tile):
    lane = lax.broadcasted_iota(jnp.int32, tile.shape, 1)
    for step in (1, 2, 4):
        other = jnp.where(
            (lane & step) == 0, pltpu.roll(tile, 128 - step, 1), pltpu.roll(tile, step, 1)
        )
        tile = tile + other
    return tile


def kernel(
    coarse, gain, bias, w_hbm, cot, dec, gw, aff,
    w, wsem, wc, st, st1, st2, at, at1, at2,
    xraw, xf, xe, hc, acts, pad0, pad1, a_t,
    cpart, cedge, ce, ch, cf, s_buf, g_buf, r_buf, ag_s, ag_r, d_buf, ssem, rsem,
):
    tm, h = lax.axis_index("tm"), lax.axis_index("height")
    core = lax.rem(tm, 2)
    t = tm // 2
    left, right = lax.rem(h + 7, 8), lax.rem(h + 1, 8)
    t_off = lax.rem(t + 7 + 2 * core, 8)
    pair = tm + 1 - 2 * core

    def send(src, dst, kind, to_tm, to_h):
        pltpu.make_async_remote_copy(
            src_ref=src, dst_ref=dst, send_sem=ssem.at[kind], recv_sem=rsem.at[kind],
            device_id=(to_tm, to_h), device_id_type=MESH,
        ).start()

    def arrived(kind, like):
        pltpu.make_async_copy(like, like, rsem.at[kind]).wait()

    def sent(kind, like):
        pltpu.make_async_copy(like, like, ssem.at[kind]).wait()

    fetch_w = pltpu.make_async_copy(w_hbm, w, wsem)
    fetch_w.start()

    barrier = pltpu.get_barrier_semaphore()

    def greet(to_tm, to_h):
        pl.semaphore_signal(barrier, inc=1, device_id=(to_tm, to_h), device_id_type=MESH)

    @pl.loop(1, 8)
    def _(k):
        greet(tm, lax.rem(h + k, 8))

    @pl.loop(1, 16)
    def _(k):
        greet(lax.rem(tm + k, 16), h)

    greet(pair, left)
    greet(pair, right)

    @pl.loop(0, 4)
    def _(k):
        to_tm = lax.rem(t + 7 + 2 * (k // 2), 8) * 2 + lax.rem(k, 2)
        greet(to_tm, left)
        greet(to_tm, right)

    x = coarse[...].astype(F32).reshape(256, 256)
    total = jnp.sum(x, axis=0, keepdims=True)
    squares = jnp.sum(x * x, axis=0, keepdims=True)
    st[...] = jnp.zeros((8, 128), F32)
    st[0:1, :] = total[:, :128]
    st[1:2, :] = total[:, 128:]
    st[2:3, :] = squares[:, :128]
    st[3:4, :] = squares[:, 128:]

    def cell(j, f):
        return pl.multiple_of((j * 8 + f) * 48, 8)

    for r in range(4):
        for f in range(8):
            cf[pl.ds(cell(1 + 4 * core + r, f) + 8, 32), :] = cot[f, r].astype(F32)
    for r in range(4):
        base = cell(1 + 4 * core + r, 0)
        ce[0, r] = cf[pl.ds(base + 8, 8, stride=48), :]
        ce[1, r] = cf[pl.ds(base + 39, 8, stride=48), :]
    hc[0, 4 - 3 * core] = jnp.zeros((8, 256), F32)
    hc[1, 4 - 3 * core] = jnp.zeros((8, 256), F32)
    acts[:, 0:2] = jnp.zeros((3, 2, 6, 16, 256), BF16)
    s_buf[:, 8:10] = jnp.zeros((9, 2, 4, 16, 128), BF16)

    pl.semaphore_wait(barrier, 32)

    @pl.loop(1, 8)
    def _(k):
        send(st, st1.at[h], STATS1, tm, lax.rem(h + k, 8))

    @pl.loop(1, 8)
    def _(k):
        to_h = lax.rem(h + k, 8)
        send(
            coarse.at[:, pl.ds(pl.multiple_of(to_h * 16, 16), 16), :],
            xraw.at[h, pl.ds(1 + 2 * core, 2)], BLOCKS, tm, to_h,
        )

    send(cot, cpart, COT_PAIR, pair, h)
    for c2 in range(2):
        send(cot.at[:, pl.ds(3 * core, 1)], cedge.at[1 - core], COT_ROWS, t_off * 2 + c2, h)
    for side, to_h in ((0, left), (1, right)):
        for c2 in range(2):
            send(ce.at[side], ch.at[1 - side, pl.ds(1 + 4 * core, 4)], COT_COLS, 2 * t + c2, to_h)
            send(ce.at[side, pl.ds(3 * core, 1)], ch.at[1 - side, pl.ds(9 - 9 * core, 1)], COT_COLS, t_off * 2 + c2, to_h)

    st1[h] = st[...]
    xraw[h, pl.ds(1 + 2 * core, 2)] = coarse[:, pl.ds(pl.multiple_of(h * 16, 16), 16), :]

    arrived(STATS1, st1.at[pl.ds(0, 7)])
    at[...] = jnp.sum(st1[...], axis=0)

    @pl.loop(1, 16)
    def _(k):
        send(at, st2.at[tm], STATS2, lax.rem(tm + k, 16), h)

    st2[tm] = at[...]

    arrived(BLOCKS, xraw.at[pl.ds(0, 7), pl.ds(0, 2)])
    own = xraw.at[:, pl.ds(1 + 2 * core, 2)]
    send(own, own, X_PAIR, pair, h)
    send(xraw.at[:, pl.ds(1 + 3 * core, 1)], xraw.at[:, pl.ds(5 - 5 * core, 1)], X_ROWS, t_off * 2 + 1 - core, h)
    for r in range(2):
        rows = xraw[:, 1 + 2 * core + r].astype(F32).reshape(128, 256)
        for half in range(2):
            xf[half, :, :] = rows[:, 128 * half : 128 * half + 128]
            for side, column in ((0, 0), (1, 15)):
                xe[side, r, :, 128 * half : 128 * half + 128] = xf.at[half][pl.ds(column, 8, stride=16), :]
    for side, to_h in ((0, left), (1, right)):
        send(xe.at[side], hc.at[1 - side, pl.ds(1 + 2 * core, 2)], X_COLS, tm, to_h)
        send(xe.at[side, pl.ds(1 - core, 1)], hc.at[1 - side, pl.ds(2 + core, 1)], X_COLS, pair, to_h)
        send(xe.at[side, pl.ds(core, 1)], hc.at[1 - side, pl.ds(5 - 5 * core, 1)], X_COLS, t_off * 2 + 1 - core, to_h)

    fetch_w.wait()

    @pl.loop(0, 48)
    def _(step):
        a = step // 16
        rows = pl.ds(pl.multiple_of(lax.rem(step, 16) * 16, 16), 16)
        taps = [[w[a * 9 + b * 3 + e, rows, :].astype(F32) for e in range(3)] for b in range(3)]
        for rc, bs in enumerate(((0,), (1, 2), (0, 1), (2,))):
            line = [taps[bs[0]][e] if len(bs) == 1 else taps[bs[0]][e] + taps[bs[1]][e] for e in range(3)]
            for cc, value in enumerate((line[0], line[1] + line[2], line[0] + line[1], line[2])):
                wc[a, rc, rows, 128 * cc : 128 * cc + 128] = value.astype(BF16)

    arrived(COT_PAIR, cpart)
    arrived(COT_ROWS, cedge)
    arrived(COT_COLS, ch)
    for r in range(4):
        for f in range(8):
            cf[pl.ds(cell(5 - 4 * core + r, f) + 8, 32), :] = cpart[f, r].astype(F32)
    top, bottom = t > 0, t < CHIPS - 1
    for f in range(8):
        cf[pl.ds(cell(0, f) + 8, 32), :] = jnp.where(top, cedge[0, f, 0].astype(F32), 0.0)
        cf[pl.ds(cell(9, f) + 8, 32), :] = jnp.where(bottom, cedge[1, f, 0].astype(F32), 0.0)
    for j in range(10):
        keep = (h > 0, h < HEIGHT - 1)
        if j == 0:
            keep = tuple(jnp.logical_and(k, top) for k in keep)
        if j == 9:
            keep = tuple(jnp.logical_and(k, bottom) for k in keep)
        cf[pl.ds(j * 384 + 7, 8, stride=48), :] = jnp.where(keep[0], ch[0, j], 0.0)
        cf[pl.ds(j * 384 + 40, 8, stride=48), :] = jnp.where(keep[1], ch[1, j], 0.0)

    @pl.loop(0, 8)
    def _(f):
        sums = []
        for j in range(10):
            base = cell(j, f)
            cols = [cf[pl.ds(base + 7 + i, 16, stride=2), :] for i in range(4)]
            sums.append((cols[2] + cols[3], cols[1] + cols[2], cols[0] + cols[1]))
        for b in range(3):
            for e in range(3):
                for row in range(4):
                    s_buf[b * 3 + e, f, row] = (sums[2 * row + 2 - b][e] + sums[2 * row + 3 - b][e]).astype(BF16)

    arrived(STATS2, st2.at[pl.ds(0, 15)])
    stats = group_totals(jnp.sum(st2[...], axis=0)) / NUMBERS
    mean = jnp.concatenate([stats[0:1], stats[1:2]], axis=1)
    square = jnp.concatenate([stats[2:3], stats[3:4]], axis=1)
    inverse = lax.rsqrt(square - mean * mean + EPSILON)
    scale, shift = inverse * gain[...], bias[...]

    def activate(v):
        shifted = (v - mean) * scale + shift
        return shifted * jax.nn.sigmoid(shifted)

    arrived(X_PAIR, xraw.at[:, pl.ds(0, 2)])
    arrived(X_ROWS, xraw.at[:, pl.ds(0, 1)])
    arrived(X_COLS, hc.at[:, pl.ds(0, 4)])

    pads = (pad0, pad1)

    @pl.loop(0, 5)
    def _(k):
        j = core + k
        inside = jnp.logical_and(jnp.logical_or(t > 0, j > 0), jnp.logical_or(t < CHIPS - 1, j < 5))
        act = activate(xraw[:, j].astype(F32).reshape(128, 256))
        act = jnp.where(inside, act, 0.0)
        act_l = jnp.where(jnp.logical_and(inside, h > 0), activate(hc[0, j]), 0.0)
        act_r = jnp.where(jnp.logical_and(inside, h < HEIGHT - 1), activate(hc[1, j]), 0.0)
        acts[1, 2:10, j] = act.astype(BF16).reshape(8, 16, 256)
        for half in range(2):
            lanes = slice(128 * half, 128 * half + 128)
            pad = pads[half]
            for f in range(8):
                pad[32 * f + 8 : 32 * f + 24, :] = act[16 * f : 16 * f + 16, lanes]
            pad[pl.ds(7, 8, stride=32), :] = act_l[:, lanes]
            pad[pl.ds(24, 8, stride=32), :] = act_r[:, lanes]
            for f in range(8):
                acts[0, 2 + f, j, :, lanes] = pad[32 * f + 7 : 32 * f + 23, :].astype(BF16)
                acts[2, 2 + f, j, :, lanes] = pad[32 * f + 9 : 32 * f + 25, :].astype(BF16)

    turned = jnp.transpose(acts[1, 2:10, 1:5].reshape(512, 256))
    a_t[...] = turned.reshape(8, 2, 16, 512)

    def part(to_h):
        lhs = a_t[:, core].reshape(128, 512)
        first = (27 * to_h) // 8
        for two in range(2):
            rhs = []
            for i in range(2):
                tap = first + 2 * two + i
                rhs.append(s_buf[lax.rem(tap, 9), pl.ds(2 - tap // 9, 8)].reshape(512, 128))
            out = jnp.dot(lhs, jnp.concatenate(rhs, axis=1), preferred_element_type=F32)
            for i in range(2):
                g_buf[to_h, :, 2 * two + i] = out[:, 128 * i : 128 * i + 128].astype(BF16).reshape(8, 16, 128)

    def send_part(to_t, to_h):
        send(g_buf.at[to_h, to_t], r_buf.at[t * 8 + h], REDUCE, to_t * 2 + core, to_h)

    @pl.loop(1, 8)
    def _(k):
        to_h = lax.rem(h + k, 8)
        part(to_h)

        @pl.loop(0, 8)
        def _(u):
            send_part(lax.rem(t + u, 8), to_h)

    part(h)

    @pl.loop(1, 8)
    def _(u):
        send_part(lax.rem(t + u, 8), h)

    r_buf[t * 8 + h] = g_buf[h, t]

    grad = jnp.zeros((256, 256), F32)
    for first in range(0, 27, 2):
        taps = range(first, min(first + 2, 27))
        lhs = [s_buf[n % 9, 2 - n // 9 : 10 - n // 9, pl.ds(2 * core, 2)].reshape(256, 128) for n in taps]
        rhs = [w[n] for n in taps]
        if len(lhs) == 2:
            lhs, rhs = [jnp.concatenate(lhs, axis=1)], [jnp.concatenate(rhs, axis=1)]
        grad = grad + lax.dot_general(lhs[0], rhs[0], (((1,), (1,)), ((), ())), preferred_element_type=F32)
    normed = (xraw[:, pl.ds(1 + 2 * core, 2)].astype(F32).reshape(256, 256) - mean) * inverse
    shifted = normed * gain[...] + shift
    sig = jax.nn.sigmoid(shifted)
    grad = grad * sig * (1.0 + shifted * (1.0 - sig))
    d_gain = jnp.sum(grad * normed, axis=0, keepdims=True)
    d_bias = jnp.sum(grad, axis=0, keepdims=True)
    sent(STATS1, st1.at[pl.ds(0, 7)])
    st[0:1, :] = d_gain[:, :128]
    st[1:2, :] = d_gain[:, 128:]
    st[2:3, :] = d_bias[:, :128]
    st[3:4, :] = d_bias[:, 128:]

    @pl.loop(1, 8)
    def _(k):
        send(st, at1.at[h], AFF1, tm, lax.rem(h + k, 8))

    at1[h] = st[...]

    for p in range(2):
        even = jnp.zeros((256, 128), F32)
        odd = jnp.zeros((256, 128), F32)
        for rc, dr in ((0, -1), (1, 0)) if p == 0 else ((2, 0), (3, 1)):
            for a in range(3):
                lhs = [acts[dc, a : a + 8, pl.ds(2 * core + 1 + dr, 2)].reshape(256, 256) for dc in range(3)]
                both = jnp.dot(lhs[1], wc[a, rc, :, 128:384], preferred_element_type=F32)
                even = even + both[:, :128] + jnp.dot(lhs[0], wc[a, rc, :, 0:128], preferred_element_type=F32)
                odd = odd + both[:, 128:] + jnp.dot(lhs[2], wc[a, rc, :, 384:512], preferred_element_type=F32)
        for f in range(8):
            for row in range(2):
                at_row = (f * 4 + 2 * row + p) * 32
                here = (f * 2 + row) * 16
                d_buf[pl.ds(at_row, 16, stride=2), :] = even[here : here + 16]
                d_buf[pl.ds(at_row + 1, 16, stride=2), :] = odd[here : here + 16]
    dec[...] = d_buf[...].astype(BF16).reshape(8, 4, 32, 128)

    arrived(AFF1, at1.at[pl.ds(0, 7)])
    sent(STATS2, st2.at[pl.ds(0, 15)])
    at[...] = jnp.sum(at1[...], axis=0)

    @pl.loop(1, 16)
    def _(k):
        send(at, at2.at[tm], AFF2, lax.rem(tm + k, 16), h)

    at2[tm] = at[...]

    arrived(REDUCE, r_buf.at[pl.ds(0, 63)])
    ag_s[...] = jnp.sum(r_buf[...].astype(F32), axis=0)

    @pl.loop(1, 8)
    def _(k):
        send(ag_s, ag_r.at[h], GATHER, tm, lax.rem(h + k, 8))

    ag_r[h] = ag_s[...]

    arrived(AFF2, at2.at[pl.ds(0, 15)])
    total = jnp.sum(at2[...], axis=0)
    aff[0:1, 0:128] = total[0:1]
    aff[0:1, 128:256] = total[1:2]
    aff[1:2, 0:128] = total[2:3]
    aff[1:2, 128:256] = total[3:4]

    arrived(GATHER, ag_r.at[pl.ds(0, 7)])
    for k in range(8):
        first = (27 * k) // 8
        gw[first : first + 4] = ag_r[k]

    sent(BLOCKS, xraw.at[pl.ds(0, 7), pl.ds(0, 2)])
    sent(COT_PAIR, cpart)
    sent(COT_ROWS, cedge)
    sent(COT_COLS, ch)
    sent(X_PAIR, xraw.at[:, pl.ds(0, 2)])
    sent(X_ROWS, xraw.at[:, pl.ds(0, 1)])
    sent(X_COLS, hc.at[:, pl.ds(0, 4)])
    sent(REDUCE, r_buf.at[pl.ds(0, 63)])
    sent(GATHER, ag_r.at[pl.ds(0, 7)])
    sent(AFF1, at1.at[pl.ds(0, 7)])
    sent(AFF2, at2.at[pl.ds(0, 15)])


def per_device(coarse, gain, bias, weight, cotangent):
    taps = jnp.transpose(weight, (1, 2, 3, 0, 4)).reshape(27, 256, 128)
    vmem = pl.BlockSpec(memory_space=pltpu.VMEM)
    vm = pltpu.VMEM
    decoded, grad_weight, grad_affine = pl.pallas_call(
        kernel,
        out_shape=(
            jax.ShapeDtypeStruct((8, 4, 32, 128), BF16),
            jax.ShapeDtypeStruct((27, 16, 128), F32),
            jax.ShapeDtypeStruct((2, 256), F32),
        ),
        in_specs=[vmem, vmem, vmem, pl.BlockSpec(memory_space=pl.ANY), vmem],
        out_specs=(vmem, vmem, vmem),
        scratch_shapes=[
            vm((27, 256, 128), BF16),
            pltpu.SemaphoreType.DMA,
            vm((3, 4, 256, 512), BF16),
            vm((8, 128), F32),
            vm((8, 8, 128), F32),
            vm((16, 8, 128), F32),
            vm((8, 128), F32),
            vm((8, 8, 128), F32),
            vm((16, 8, 128), F32),
            vm((8, 6, 16, 256), BF16),
            vm((2, 128, 128), F32),
            vm((2, 2, 8, 256), F32),
            vm((2, 6, 8, 256), F32),
            vm((3, 10, 6, 16, 256), BF16),
            vm((256, 128), F32),
            vm((256, 128), F32),
            vm((8, 2, 16, 512), BF16),
            vm((8, 4, 32, 128), BF16),
            vm((2, 8, 1, 32, 128), BF16),
            vm((2, 4, 8, 128), F32),
            vm((2, 10, 8, 128), F32),
            vm((10 * 8 * 48, 128), F32),
            vm((9, 10, 4, 16, 128), BF16),
            vm((8, 8, 4, 16, 128), BF16),
            vm((64, 4, 16, 128), BF16),
            vm((4, 16, 128), F32),
            vm((8, 4, 16, 128), F32),
            vm((1024, 128), F32),
            pltpu.SemaphoreType.DMA((13,)),
            pltpu.SemaphoreType.DMA((13,)),
        ],
        compiler_params=pltpu.CompilerParams(
            collective_id=0, has_side_effects=True, vmem_limit_bytes=48 * 2**20
        ),
        cost_estimate=pl.CostEstimate(flops=2 * 10**9, bytes_accessed=4 * 10**6, transcendentals=300000),
    )(coarse.reshape(2, 128, 256), gain.reshape(1, 256), bias.reshape(1, 256), taps, cotangent)
    grad_weight = jnp.transpose(grad_weight.reshape(3, 3, 3, 16, 128), (3, 0, 1, 2, 4))
    return decoded, grad_weight, grad_affine


def solution(mesh):
    return jax.shard_map(
        per_device,
        mesh=mesh,
        in_specs=(P("height", "tm", None, None), P(), P(), P(), P(None, "tm", "height", None)),
        out_specs=(P(None, "tm", "height", None), P("tm", None, None, None, None), P()),
        check_vma=False,
    )
```

time: 412 us -> 49.6 us (0.12)
  blocking collectives: 148 us -> 0 us
  waiting for transfers between devices: 142 us -> 0 us
  matrix products: 45.5 us -> 0 us
  Pallas kernels: 0 us -> 42.1 us
  starting transfers between devices: 27 us -> 0 us
  local copies, waits for them, and re-layouts: 26.8 us -> 6.65 us
  between operations: 14.8 us -> 0.65 us
  other arithmetic: 6.43 us -> 0 us
    psum x2 -> x0, blocking collectives: 138 us -> none  [the longest x1 72.6 us: per_device(): lax.psum((partial_sums[0], partial_sums[1]), ('tm', 'height'))]
    psum x1 -> x0, waiting for transfers between devices: 72 us -> none  [per_device(): lax.psum(jnp.stack(pieces, axis=1).reshape(channels_in, 3, 3, 3, channels...]
    reduce_scatter x1 -> x0, waiting for transfers between devices: 64.3 us -> none  [per_device(): lax.psum_scatter(full_term, 'tm', scatter_dimension=0, tiled=True)]
    dot_general x81 -> x0, matrix products: 45.5 us -> none  [the longest x27 26.7 us: per_device(): lax.dot_general(window, flat_cot, (((0,), (0,)), ((), ())), preferred_ele...]
    pallas_call x0 -> x1, Pallas kernels: none -> 42.1 us  [per_device(): pl.pallas_call(kernel, out_shape=(jax.ShapeDtypeStruct((8, 4, 32, 128), B...]
    ppermute x8 -> x0, starting transfers between devices: 18.6 us -> none  [the longest x4 13.4 us: extended_2(): lax.ppermute(lax.slice_in_dim(block, block.shape[dim] - width, None, axis...]
    all_to_all x1 -> x0, blocking collectives: 10 us -> none  [per_device(): lax.all_to_all(jax.nn.silu(shifted).astype(jnp.bfloat16), 'height', split...]
    slice x7 -> x0, local copies, waits for them, and re-layouts: 9.72 us -> none  [the longest x2 7.01 us: per_device(): upsampled[tap_t:tap_t + frames_here, tap_r:tap_r + rows_here, tap_c:tap_c...]
  transfers between devices with their start and end apart: 11 -> 0, of which waited for: 5 -> 0; matrix products, arithmetic and copies ran while one was open for 3% -> 0% of each run, Pallas kernels for 0% -> 0%
where the time goes in v1:
time: 49.6 us; the launch traced here: 49.4 us
  Pallas kernels  42.1 us (85%)
  local copies, waits for them, and re-layouts  6.65 us (13%)
  between operations  0.65 us (1%)
    pallas_call x1, Pallas kernels, per_device(): pl.pallas_call(kernel, out_shape=(jax.ShapeDtypeStruct((8, 4, 32, 128), B...  42.1 us
    unnamed x13, local copies, waits for them, and re-layouts  6.65 us

profile of v1, /device:TPU:0, one launch (start us, length us, event | category | flops | bytes accessed | tf_op | source)
XLA Modules:
  0.0 49.4 jit_solution(12985481152960894007)
XLA Ops:
  0.6 0.0 copy-start
  0.6 1.5 %copy-done = bf16[256,3,3,3,128]{4,0,3,2,1:T(8,128)(2,1)S(1)} copy-done((bf16[256,3,3,3,128]{4,0,3,2,1:T(8,128)(2,1)S(1)}, bf16[256,3,3,3,128]{4,0,3,2,1:T(8,128)(2,1)}, u32[]{:S(2)}) %copy-start) | copy-done | bytes 1769496
  2.1 0.0 copy-start.1
  2.1 0.9 %copy-done.1 = bf16[8,4,32,128]{3,2,1,0:T(8,128)(2,1)S(1)} copy-done((bf16[8,4,32,128]{3,2,1,0:T(8,128)(2,1)S(1)}, bf16[8,4,32,128]{3,2,1,0:T(8,128)(2,1)}, u32[]{:S(2)}) %copy-start.1) | copy-done | bytes 262168
  3.1 0.0 copy-start.2
  3.1 0.9 %copy-done.2 = bf16[1,2,128,256]{3,2,1,0:T(8,128)(2,1)S(1)} copy-done((bf16[1,2,128,256]{3,2,1,0:T(8,128)(2,1)S(1)}, bf16[1,2,128,256]{3,2,1,0:T(8,128)(2,1)}, u32[]{:S(2)}) %copy-start.2) | copy-done | bytes 131096
  4.0 0.0 copy-start.3
  4.0 0.7 %copy-done.3 = f32[256]{0:T(256)S(1)} copy-done((f32[256]{0:T(256)S(1)}, f32[256]{0:T(256)}, u32[]{:S(2)}) %copy-start.3) | copy-done | bytes 1048
  4.6 0.0 copy-start.4
  4.6 0.7 %copy-done.4 = f32[256]{0:T(256)S(1)} copy-done((f32[256]{0:T(256)S(1)}, f32[256]{0:T(256)}, u32[]{:S(2)}) %copy-start.4) | copy-done | bytes 1048
  5.3 42.1 %shard_map.76 = (bf16[8,4,32,128]{3,2,1,0:T(8,128)(2,1)S(1)}, f32[27,16,128]{2,1,0:T(8,128)S(1)}, f32[2,256]{1,0:T(2,128)S(1)}) custom-call(bf16[2,128,256]{2,1,0:T(8,128)(2,1)S(1)} %bitcast.11, f32[1,256]{1,0:T(1,128)S(1)} %bitcast.12, f32[1,256]{1,0:T(1,128)S(1)} %bitcast.13, bf16[27,256,128]{2,1,0:T(8,128)(2,1)S(1)} %bitcast.10, ...), custom_call_target="tpu_custom_call" | custom-call | flops 2000000000 | bytes 4000000 | tf_op jit(solution)/shard_map/pallas_call | solution.py:358
  47.4 0.7 %copy.11 = bf16[8,4,32,128]{3,2,1,0:T(8,128)(2,1)} copy(bf16[8,4,32,128]{3,2,1,0:T(8,128)(2,1)S(1)} %get-tuple-element.12) | data formatting | bytes 524288
  48.1 0.7 %copy.12 = f32[16,3,3,3,128]{4,0,3,2,1:T(8,128)} copy(f32[16,3,3,3,128]{4,0,3,2,1:T(8,128)S(1)} %bitcast.9) | data formatting | bytes 442368
  48.8 0.6 %copy.13 = f32[2,256]{1,0:T(2,128)} copy(f32[2,256]{1,0:T(2,128)S(1)} %get-tuple-element.14) | data formatting | bytes 4096
Async XLA Ops:
  0.6 1.5 %copy-start = (bf16[256,3,3,3,128]{4,0,3,2,1:T(8,128)(2,1)S(1)}, bf16[256,3,3,3,128]{4,0,3,2,1:T(8,128)(2,1)}, u32[]{:S(2)}) copy-start(bf16[256,3,3,3,128]{4,0,3,2,1:T(8,128)(2,1)} %param.8) | copy-start | bytes 5308420
  2.1 0.9 %copy-start.1 = (bf16[8,4,32,128]{3,2,1,0:T(8,128)(2,1)S(1)}, bf16[8,4,32,128]{3,2,1,0:T(8,128)(2,1)}, u32[]{:S(2)}) copy-start(bf16[8,4,32,128]{3,2,1,0:T(8,128)(2,1)} %cot.1) | copy-start | bytes 786436
  3.1 0.9 %copy-start.2 = (bf16[1,2,128,256]{3,2,1,0:T(8,128)(2,1)S(1)}, bf16[1,2,128,256]{3,2,1,0:T(8,128)(2,1)}, u32[]{:S(2)}) copy-start(bf16[1,2,128,256]{3,2,1,0:T(8,128)(2,1)} %param.5) | copy-start | bytes 393220
  4.0 0.7 %copy-start.3 = (f32[256]{0:T(256)S(1)}, f32[256]{0:T(256)}, u32[]{:S(2)}) copy-start(f32[256]{0:T(256)} %param.6) | copy-start | bytes 3076
  4.6 0.7 %copy-start.4 = (f32[256]{0:T(256)S(1)}, f32[256]{0:T(256)}, u32[]{:S(2)}) copy-start(f32[256]{0:T(256)} %param.7) | copy-start | bytes 3076
